TPU v7x, 32 devices: a whole 2x2x4 slice. The times are simulated.
32 devices in a mesh: ctx: 16 (over z, y, core), tp: 2 (over x).
Axes of the slice: x: 2, y: 2, z: 4, core: 2. Of those that a mesh axis runs over, the one named last changes fastest.
Arguments:
- queries: bfloat16 [8192, 4096], P('ctx', 'tp'), may hold values from -0.19921875 to 0.19921875
- keys: bfloat16 [8192, 4096], P('ctx', 'tp'), may hold values from -0.19921875 to 0.19921875
- values: bfloat16 [8192, 4096], P('ctx', 'tp'), may hold values from -0.19921875 to 0.19921875
- cotangent: bfloat16 [8192, 2048], P('ctx', 'tp'), may hold values from -6 to 6
- out_weight: bfloat16 [4096, 2048], P('tp'), may hold values from -0.125 to 0.125
- memory: float32 [32, 128, 128], P('tp'), may hold values from -0.6 to 0.6
Outputs:
- query_grad: bfloat16 [8192, 4096], P('ctx', 'tp')
- key_grad: bfloat16 [8192, 4096], P('ctx', 'tp')
- value_grad: bfloat16 [8192, 4096], P('ctx', 'tp')
- weight_grad: float32 [4096, 2048], P(('tp', 'ctx'))
All inputs are finite; a program needn't handle non-finite values.
Results may differ from a plain program's by a relative error of at most 0.0058.
Values may be sent and summed in bfloat16 or wider, within the bound.
No kernel may reach another device: no remote copies, remote signals or barrier semaphores. Data moves between devices by JAX's collectives and lax.ppermute only.
A program may use at most 320 MiB of HBM per device.

v0:
```python
import jax
import jax.numpy as jnp
from jax import lax
from jax.sharding import PartitionSpec as P


def carried_in(value, axis, combine, identity, reverse):
    peers, index = (lax.axis_size(axis), lax.axis_index(axis))
    everything = lax.all_gather(value, axis)
    start = jnp.broadcast_to(jnp.asarray(identity, value.dtype), value.shape)

    def lap(k, before):
        at = peers - 1 - k if reverse else k
        reached = at > index if reverse else at < index
        new = combine(before, everything[at])
        return jnp.where(reached, new, before)

    return lax.fori_loop(0, peers, lap, start)


def add_pair(earlier, later):
    return earlier + later


def local(queries, keys, values, cotangent, out_weight, memory):
    tok_rows, col_width = queries.shape
    heads = memory.shape[0]
    head_size = memory.shape[1]
    full_cot = lax.all_gather(cotangent, "tp", axis=1, tiled=True)
    out_grad = lax.dot_general(
        full_cot, out_weight, (((1,), (1,)), ((), ())), preferred_element_type=jnp.float32
    ).astype(jnp.bfloat16)
    query_heads = queries.reshape(tok_rows, heads, head_size)
    key_heads = keys.reshape(tok_rows, heads, head_size)
    value_heads = values.reshape(tok_rows, heads, head_size)
    grad_heads = out_grad.reshape(tok_rows, heads, head_size)
    kv_sum = jnp.einsum("the,thf->hef", key_heads, value_heads, preferred_element_type=jnp.float32)
    qd_sum = jnp.einsum("the,thf->hef", query_heads, grad_heads, preferred_element_type=jnp.float32)
    zeros = jnp.zeros_like(kv_sum)
    before = carried_in(kv_sum, "ctx", add_pair, zeros, False)
    after = carried_in(qd_sum, "ctx", add_pair, zeros, True)
    state = (memory + before).astype(jnp.bfloat16)
    adjoint = after.astype(jnp.bfloat16)
    causal = lax.broadcasted_iota(jnp.int32, (tok_rows, tok_rows), 0) >= lax.broadcasted_iota(
        jnp.int32, (tok_rows, tok_rows), 1
    )
    scores = jnp.einsum("the,she->hts", query_heads, key_heads, preferred_element_type=jnp.float32)
    scores = jnp.where(causal[None], scores, 0.0).astype(jnp.bfloat16)
    dscores = jnp.einsum(
        "thf,shf->hts", grad_heads, value_heads, preferred_element_type=jnp.float32
    )
    dscores = jnp.where(causal[None], dscores, 0.0).astype(jnp.bfloat16)
    attended = jnp.einsum(
        "the,hef->thf", query_heads, state, preferred_element_type=jnp.float32
    ) + jnp.einsum("hts,shf->thf", scores, value_heads, preferred_element_type=jnp.float32)
    attended = attended.astype(jnp.bfloat16).reshape(tok_rows, col_width)
    query_g = jnp.einsum(
        "thf,hef->the", grad_heads, state, preferred_element_type=jnp.float32
    ) + jnp.einsum("hts,she->the", dscores, key_heads, preferred_element_type=jnp.float32)
    key_g = jnp.einsum(
        "shf,hef->she", value_heads, adjoint, preferred_element_type=jnp.float32
    ) + jnp.einsum("hts,the->she", dscores, query_heads, preferred_element_type=jnp.float32)
    value_g = jnp.einsum(
        "she,hef->shf", key_heads, adjoint, preferred_element_type=jnp.float32
    ) + jnp.einsum("hts,thf->shf", scores, grad_heads, preferred_element_type=jnp.float32)
    weight_grad = lax.psum_scatter(
        lax.dot_general(
            attended, full_cot, (((0,), (0,)), ((), ())), preferred_element_type=jnp.float32
        ),
        "ctx",
        scatter_dimension=0,
        tiled=True,
    )
    return (
        query_g.astype(jnp.bfloat16).reshape(tok_rows, col_width),
        key_g.astype(jnp.bfloat16).reshape(tok_rows, col_width),
        value_g.astype(jnp.bfloat16).reshape(tok_rows, col_width),
        weight_grad,
    )


def solution(mesh):
    in_specs = (
        P("ctx", "tp"),
        P("ctx", "tp"),
        P("ctx", "tp"),
        P("ctx", "tp"),
        P("tp", None),
        P("tp", None, None),
    )
    out_specs = (P("ctx", "tp"), P("ctx", "tp"), P("ctx", "tp"), P(("tp", "ctx"), None))
    return jax.shard_map(local, mesh=mesh, in_specs=in_specs, out_specs=out_specs, check_vma=False)
```

profile of v0, /device:TPU:0, one launch (start us, length us, event | category | flops | bytes accessed | tf_op | source)
XLA Modules:
  0.0 490.1 jit_solution(12181195111728248671)
XLA Ops:
  8.0 3.9 copy.56
  11.9 4.0 fusion.10
  15.9 29.5 %all-gather.6.cloned.1.call-done = bf16[512,2048]{1,0:T(8,128)(2,1)} async-done(((bf16[512,1024]{1,0:T(8,128)(2,1)}), bf16[512,2048]{1,0:T(8,128)(2,1)}) %all-gather.6.cloned.1.call-update) | async-done | bytes 2097168 | tf_op jit(solution)/shard_map/all_gather | solution.py:29
  45.4 9.9 %convolution_convert_fusion = bf16[512,2048]{1,0:T(8,128)(2,1)} fusion(bf16[512,2048]{1,0:T(8,128)(2,1)} %all-gather.6.cloned.1.call-done, bf16[2048,2048]{1,0:T(8,128)(2,1)} %param.14), kind=kOutput, calls=%fused_computation.11 | convolution fusion | flops 4296015872 | bytes 12582912 | tf_op jit(solution)/shard_map/dot_general | solution.py:30
  55.3 4.1 copy.57
  59.3 2.3 fusion.15
  63.2 7.2 %select_convert_fusion = bf16[16,512,512]{2,1,0:T(8,128)(2,1)} fusion(pred[512,512]{1,0:T(8,128)(4,1)S(1)} %iota_compare_fusion, bf16[512,2048]{1,0:T(8,128)(2,1)S(1)} %copy-done, bf16[512,2048]{1,0:T(8,128)(2,1)} %param.11), kind=kOutput, calls=%fused_computation.2 | convolution fusion | flops 1082130432 | bytes 12845056 | tf_op jit(solution)/shard_map/the,she->hts/dot_general | solution.py:47
  70.4 104.7 %all-gather.8.cloned.1.call-done = f32[256,128,128]{2,1,0:T(8,128)} async-done(((f32[16,128,128]{2,1,0:T(8,128)}), f32[256,128,128]{2,1,0:T(8,128)}) %all-gather.8.cloned.1.call-update) | async-done | bytes 16777232 | tf_op jit(solution)/shard_map/all_gather | solution.py:9
  175.1 26.2 %while.30 = (s32[]{:T(128)}, f32[16,128,128]{2,1,0:T(8,128)S(1)}, s32[]{:T(128)}, f32[16,16,128,128]{3,2,1,0:T(8,128)}, s32[]{:T(128)}, /*index=5*/s32[]{:T(128)}) while((s32[]{:T(128)}, f32[16,128,128]{2,1,0:T(8,128)S(1)}, s32[]{:T(128)}, f32[16,16,128,128]{3,2,1,0:T(8,128)}, s32[]{:T(128)}, /*index=5*/s32[]{:T(128)}) %tuple.89), condition=%wide.region_1.2_spmd.clone, body=%wide.region_0.1_spmd.clone.sunk | while | flops 786436 | bytes 3145829 | solution.py:18
  176.7 1.6 add_select_fusion.4
  179.9 1.6 add_select_fusion.4
  181.5 1.7 add_select_fusion.4
  183.3 1.7 add_select_fusion.4
  185.0 1.7 add_select_fusion.4
  186.7 1.6 add_select_fusion.4
  190.0 1.6 add_select_fusion.4
  191.6 1.6 add_select_fusion.4
  193.2 1.6 add_select_fusion.4
  194.8 1.6 add_select_fusion.4
  196.4 1.6 add_select_fusion.4
  198.1 1.6 add_select_fusion.4
  199.7 1.6 add_select_fusion.4
  205.1 7.6 %fusion = bf16[512,16,128]{0,2,1:T(8,128)(2,1)} fusion(f32[16,128,512]{2,1,0:T(8,128)S(1)} %fusion.4, bf16[16,512,512]{2,1,0:T(8,128)(2,1)} %select_convert_fusion, bf16[512,16,128]{0,2,1:T(8,128)(2,1)S(1)} %bitcast.105), kind=kOutput, calls=%fused_computation.5 | convolution fusion | flops 1075838976 | bytes 16777216 | tf_op jit(solution)/shard_map/hts,shf->thf/dot_general | solution.py:55
  212.6 12.5 %fusion.30 = f32[2048,2048]{1,0:T(8,128)} fusion(bf16[512,2048]{0,1:T(8,128)(2,1)} %bitcast.113, bf16[512,2048]{1,0:T(8,128)(2,1)} %all-gather.6.cloned.1.call-done), kind=kOutput, calls=%fused_computation.39 | convolution fusion | flops 4294967296 | bytes 20971520 | tf_op jit(solution)/shard_map/dot_general | solution.py:67
  225.2 8.8 %select_convert_fusion.1 = bf16[16,512,512]{2,1,0:T(8,128)(2,1)} fusion(bf16[512,16,128]{0,2,1:T(8,128)(2,1)} %bitcast.107, bf16[512,16,128]{0,2,1:T(8,128)(2,1)} %bitcast.103, pred[512,512]{1,0:T(8,128)(4,1)S(1)} %iota_compare_fusion), kind=kOutput, calls=%fused_computation.3 | convolution fusion | flops 1082130432 | bytes 12845056 | tf_op jit(solution)/shard_map/thf,shf->hts/dot_general | solution.py:49
  234.0 2.8 fusion.29
  236.7 8.8 %fusion.2 = bf16[512,16,128]{0,2,1:T(8,128)(2,1)} fusion(f32[16,128,512]{2,1,0:T(8,128)} %fusion.29, bf16[16,512,512]{2,1,0:T(8,128)(2,1)} %select_convert_fusion.1, bf16[512,2048]{1,0:T(8,128)(2,1)S(1)} %copy-done.4), kind=kOutput, calls=%fused_computation.9 | convolution fusion | flops 1075838976 | bytes 16777216 | tf_op jit(solution)/shard_map/hts,she->the/dot_general | solution.py:59
  245.5 3.9 copy.51
  249.4 52.9 %all-gather.10.cloned.1.call-done = f32[256,128,128]{2,1,0:T(8,128)} async-done(((f32[16,128,128]{2,1,0:T(8,128)}), f32[256,128,128]{2,1,0:T(8,128)}) %all-gather.10.cloned.1.call-update) | async-done | bytes 16777232 | tf_op jit(solution)/shard_map/all_gather | solution.py:9
  302.3 27.9 %while.31 = (s32[]{:T(128)}, f32[16,128,128]{2,1,0:T(8,128)S(1)}, s32[]{:T(128)}, f32[16,16,128,128]{3,2,1,0:T(8,128)}, s32[]{:T(128)}, /*index=5*/s32[]{:T(128)}, s32[]{:T(128)}, s32[]{:T(128)}) while((s32[]{:T(128)}, f32[16,128,128]{2,1,0:T(8,128)S(1)}, s32[]{:T(128)}, f32[16,16,128,128]{3,2,1,0:T(8,128)}, s32[]{:T(128)}, ...), condition=%wide.region_3.4_spmd.clone, body=%wide.region_2.3_spmd.clone.sunk | while | flops 786440 | bytes 3145891 | solution.py:18
  310.4 1.6 add_select_fusion.5
  312.1 1.8 add_select_fusion.5
  314.0 1.8 add_select_fusion.5
  315.8 1.8 add_select_fusion.5
  317.7 1.7 add_select_fusion.5
  319.4 1.8 add_select_fusion.5
  321.3 1.8 add_select_fusion.5
  323.0 1.7 add_select_fusion.5
  324.8 1.8 add_select_fusion.5
  326.6 1.7 add_select_fusion.5
  328.4 1.8 add_select_fusion.5
  330.2 2.6 fusion.27
  332.8 6.2 %fusion.1 = bf16[512,16,128]{0,2,1:T(8,128)(2,1)} fusion(f32[16,128,512]{2,1,0:T(8,128)S(1)} %fusion.27, bf16[16,512,512]{2,1,0:T(8,128)(2,1)} %select_convert_fusion.1, bf16[512,2048]{1,0:T(8,128)(2,1)S(1)} %copy-done), kind=kOutput, calls=%fused_computation.7 | convolution fusion | flops 1075838976 | bytes 16777216 | tf_op jit(solution)/shard_map/hts,the->she/dot_general | solution.py:62
  339.0 3.9 copy.52
  342.9 2.5 fusion.13
  345.4 6.2 %add_convert_fusion = bf16[16,128,512]{2,1,0:T(8,128)(2,1)} fusion(f32[16,128,512]{2,1,0:T(8,128)S(1)} %fusion.13, bf16[512,16,128]{0,2,1:T(8,128)(2,1)S(1)} %bitcast.109, bf16[16,512,512]{2,1,0:T(8,128)(2,1)} %select_convert_fusion), kind=kOutput, calls=%fused_computation.10 | convolution fusion | flops 1075838976 | bytes 16777216 | tf_op jit(solution)/shard_map/hts,thf->shf/dot_general | solution.py:65
  351.6 3.9 copy.53
  355.5 128.1 %reduce-scatter.2.cloned.1.call-done = f32[128,2048]{1,0:T(8,128)} async-done(((f32[2048,2048]{1,0:T(8,128)}), f32[128,2048]{1,0:T(8,128)}) %reduce-scatter.2.cloned.1.call-update) | async-done | bytes 1048592 | tf_op jit(solution)/shard_map/reduce_scatter | solution.py:66
  (36 shorter events, 18.8 us)
Async XLA Ops:
  7.2 52.2 %copy-start = (bf16[512,2048]{1,0:T(8,128)(2,1)S(1)}, bf16[512,2048]{1,0:T(8,128)(2,1)}, u32[]{:S(2)}) copy-start(bf16[512,2048]{1,0:T(8,128)(2,1)} %param.10) | copy-start | bytes 6291460
  7.2 38.2 %all-gather.6.cloned.1.call-start = ((), (), s32[]{:S(2)}) async-start(), calls=%async_computation.1 | async-start | bytes 3145728 | tf_op jit(solution)/shard_map/all_gather | solution.py:29
  7.9 167.2 %all-gather.8.cloned.1.call-start = ((), (), s32[]{:S(2)}) async-start(), calls=%async_computation.3 | async-start | bytes 17825792 | tf_op jit(solution)/shard_map/all_gather | solution.py:9
  15.9 286.5 %all-gather.10.cloned.1.call-start = ((), (), s32[]{:S(2)}) async-start(), calls=%async_computation.4 | async-start | bytes 17825792 | tf_op jit(solution)/shard_map/all_gather | solution.py:9
  63.0 420.6 %reduce-scatter.2.cloned.1.call-start = ((), (), s32[]{:S(2)}) async-start(), calls=%async_computation.2 | async-start | bytes 17825792 | tf_op jit(solution)/shard_map/reduce_scatter | solution.py:66
  202.6 0.8 copy-start.5
  203.4 1.6 copy-start.1
  225.2 8.8 %copy-start.2 = (bf16[512,2048]{0,1:T(8,128)(2,1)S(1)}, bf16[512,2048]{0,1:T(8,128)(2,1)}, u32[]{:S(2)}) copy-start(bf16[512,2048]{0,1:T(8,128)(2,1)} %copy.57) | copy-start | bytes 6291460
  225.2 8.8 %copy-start.6 = (bf16[16,128,128]{2,1,0:T(8,128)(2,1)S(1)}, bf16[16,128,128]{2,1,0:T(8,128)(2,1)}, u32[]{:S(2)}) copy-start(bf16[16,128,128]{2,1,0:T(8,128)(2,1)} %copy-done.5) | copy-start | bytes 1572868
  234.0 2.8 copy-start.4
  342.9 2.5 copy-start.3
Sparse Core Ops, SparseCore 0:
  9.6 35.8 all-gather.5
  48.1 126.8 all-gather.7
  177.2 125.0 all-gather.9
  306.9 176.6 reduce-scatter.1
where the time goes:
time: 492 us; the launch traced here: 490 us
  waiting for transfers between devices  316 us (64%)
  matrix products  82 us (17%)
  other arithmetic  54.7 us (11%)
  local copies, waits for them, and re-layouts  22.7 us (5%)
  between operations  13.9 us (3%)
    all_gather x2, waiting for transfers between devices, carried_in(): everything = lax.all_gather(value, axis)  158 us
    reduce_scatter x1, waiting for transfers between devices, local(): lax.psum_scatter(lax.dot_general(attended, full_cot, (((0,), (0,)), ((),...  128 us
    select_n x32, other arithmetic, lap(): return jnp.where(reached, new, before)  53.3 us
    all_gather x1, waiting for transfers between devices, local(): full_cot = lax.all_gather(cotangent, 'tp', axis=1, tiled=True)  29.5 us
    unnamed x17, local copies, waits for them, and re-layouts  13.4 us
    dot_general x1, matrix products, local(): lax.dot_general(attended, full_cot, (((0,), (0,)), ((), ())), preferred_e...  12.5 us
    dot_general x1, matrix products, local(): lax.dot_general(full_cot, out_weight, (((1,), (1,)), ((), ())), preferred...  9.87 us
  transfers between devices with their start and end apart: 4, of which 4 were waited for; matrix products, arithmetic and copies ran while one was open for 32% of the time, Pallas kernels for 0%

commit v1 on v0

v1 whole, which is shorter than its diff:
```python
import functools

import jax
import jax.numpy as jnp
from jax import lax
from jax.experimental import pallas as pl
from jax.experimental.pallas import tpu as pltpu
from jax.sharding import PartitionSpec as P

BF = jnp.bfloat16
F32 = jnp.float32
VMEM_LIMIT = 56 * 1024 * 1024


def dot(a, b, ca, cb):
    return lax.dot_general(a, b, (((ca,), (cb,)), ((), ())), preferred_element_type=F32)


def params():
    return pltpu.CompilerParams(vmem_limit_bytes=VMEM_LIMIT)


def cost(flops, nbytes):
    return pl.CostEstimate(flops=int(flops), bytes_accessed=int(nbytes), transcendentals=0)


def kv_kernel(head, a_ref, b_ref, o_ref):
    for j in range(a_ref.shape[1] // head):
        at = slice(j * head, (j + 1) * head)
        o_ref[at, :] = dot(a_ref[:, at], b_ref[:, at], 0, 0).astype(o_ref.dtype)


def block_sums(a, b, head):
    tok, width = a.shape
    step = 2 * head
    return pl.pallas_call(
        functools.partial(kv_kernel, head),
        grid=(width // step,),
        in_specs=[pl.BlockSpec((tok, step), lambda i: (0, i))] * 2,
        out_specs=pl.BlockSpec((step, head), lambda i: (i, 0)),
        out_shape=jax.ShapeDtypeStruct((width, head), BF),
        compiler_params=params(),
        cost_estimate=cost(2 * tok * width * head, 4 * tok * width),
        name="block_sums",
    )(a, b)


def masked(tok, upper):
    row = lax.broadcasted_iota(jnp.int32, (tok, tok), 0)
    col = lax.broadcasted_iota(jnp.int32, (tok, tok), 1)
    return row <= col if upper else row >= col


def causal_apply(a, b, c, upper):
    tok = a.shape[0]
    half = tok // 2
    keep = masked(half, upper)

    def tile(x, y, diagonal):
        s = dot(x, y, 1, 1)
        if diagonal:
            s = jnp.where(keep, s, 0.0)
        return s.astype(BF)

    a0, a1, b0, b1, c0, c1 = a[:half], a[half:], b[:half], b[half:], c[:half], c[half:]
    first = dot(tile(a0, b0, True), c0, 1, 0)
    second = dot(tile(a1, b1, True), c1, 1, 0)
    if upper:
        first = first + dot(tile(a0, b1, False), c1, 1, 0)
    else:
        second = second + dot(tile(a1, b0, False), c0, 1, 0)
    return first, second


def intra_kernel(head, q_ref, k_ref, v_ref, o_ref):
    half = q_ref.shape[0] // 2
    for j in range(q_ref.shape[1] // head):
        at = slice(j * head, (j + 1) * head)
        first, second = causal_apply(q_ref[:, at], k_ref[:, at], v_ref[:, at], False)
        o_ref[:half, at] = first
        o_ref[half:, at] = second


def intra(q, k, v, head):
    tok, width = q.shape
    step = 2 * head
    spec = pl.BlockSpec((tok, step), lambda i: (0, i))
    return pl.pallas_call(
        functools.partial(intra_kernel, head),
        grid=(width // step,),
        in_specs=[spec] * 3,
        out_specs=spec,
        out_shape=jax.ShapeDtypeStruct((tok, width), F32),
        compiler_params=params(),
        cost_estimate=cost(4 * tok * tok * width, 10 * tok * width),
        name="intra",
    )(q, k, v)


def grad_kernel(head, tp_ref, own_ref, far_ref, wo_ref, wf_ref, q_ref, g_ref, s_ref):
    g = dot(own_ref[...], wo_ref[...], 1, 1) + dot(far_ref[...], wf_ref[...], 1, 1)
    g = g.astype(BF)
    g_ref[...] = g
    for j in range(g.shape[1] // head):
        at = slice(j * head, (j + 1) * head)
        s_ref[at, :] = dot(q_ref[:, at], g[:, at], 0, 0).astype(s_ref.dtype)


def out_grad_and_sums(tp, own, far, w, q, head):
    tok, feat = own.shape
    width = q.shape[1]
    step = 2 * head
    whole = pl.BlockSpec((tok, feat), lambda i, t: (0, 0))
    return pl.pallas_call(
        functools.partial(grad_kernel, head),
        grid_spec=pltpu.PrefetchScalarGridSpec(
            num_scalar_prefetch=1,
            grid=(width // step,),
            in_specs=[
                whole,
                whole,
                pl.BlockSpec((step, feat), lambda i, t: (i, t[0])),
                pl.BlockSpec((step, feat), lambda i, t: (i, 1 - t[0])),
                pl.BlockSpec((tok, step), lambda i, t: (0, i)),
            ],
            out_specs=[
                pl.BlockSpec((tok, step), lambda i, t: (0, i)),
                pl.BlockSpec((step, head), lambda i, t: (i, 0)),
            ],
        ),
        out_shape=[
            jax.ShapeDtypeStruct((tok, width), BF),
            jax.ShapeDtypeStruct((width, head), BF),
        ],
        compiler_params=params(),
        cost_estimate=cost(4 * tok * feat * width, 4 * feat * width + 4 * tok * width),
        name="out_grad",
    )(tp, own, far, w, w, q)


def attended_kernel(head, q_ref, s_ref, i_ref, o_ref):
    for j in range(q_ref.shape[1] // head):
        at = slice(j * head, (j + 1) * head)
        o_ref[:, at] = (dot(q_ref[:, at], s_ref[at, :], 1, 0) + i_ref[:, at]).astype(BF)


def attended_of(q, state, inner, head):
    tok, width = q.shape
    step = 2 * head
    spec = pl.BlockSpec((tok, step), lambda i: (0, i))
    return pl.pallas_call(
        functools.partial(attended_kernel, head),
        grid=(width // step,),
        in_specs=[spec, pl.BlockSpec((step, head), lambda i: (i, 0)), spec],
        out_specs=spec,
        out_shape=jax.ShapeDtypeStruct((tok, width), BF),
        compiler_params=params(),
        cost_estimate=cost(2 * tok * head * width, 8 * tok * width),
        name="attended",
    )(q, state, inner)


def weight_kernel(a_ref, own_ref, far_ref, o_ref):
    feat = own_ref.shape[1]
    a = a_ref[...]
    o_ref[:, :feat] = dot(a, own_ref[...], 0, 0).astype(o_ref.dtype)
    o_ref[:, feat:] = dot(a, far_ref[...], 0, 0).astype(o_ref.dtype)


def weight_term(a, own, far):
    tok, width = a.shape
    feat = own.shape[1]
    step = 256
    whole = pl.BlockSpec((tok, feat), lambda i: (0, 0))
    return pl.pallas_call(
        weight_kernel,
        grid=(width // step,),
        in_specs=[pl.BlockSpec((tok, step), lambda i: (0, i)), whole, whole],
        out_specs=pl.BlockSpec((step, 2 * feat), lambda i: (i, 0)),
        out_shape=jax.ShapeDtypeStruct((width, 2 * feat), BF),
        compiler_params=params(),
        cost_estimate=cost(4 * tok * feat * width, 4 * feat * width + 2 * tok * width),
        name="weight_term",
    )(a, own, far)


def query_kernel(head, g_ref, v_ref, k_ref, s_ref, o_ref):
    half = g_ref.shape[0] // 2
    for j in range(g_ref.shape[1] // head):
        at = slice(j * head, (j + 1) * head)
        g = g_ref[:, at]
        first, second = causal_apply(g, v_ref[:, at], k_ref[:, at], False)
        carried = dot(g, s_ref[at, :], 1, 1)
        o_ref[:half, at] = (first + carried[:half]).astype(BF)
        o_ref[half:, at] = (second + carried[half:]).astype(BF)


def query_grad_of(g, v, k, state, head):
    tok, width = g.shape
    step = 2 * head
    spec = pl.BlockSpec((tok, step), lambda i: (0, i))
    return pl.pallas_call(
        functools.partial(query_kernel, head),
        grid=(width // step,),
        in_specs=[spec, spec, spec, pl.BlockSpec((step, head), lambda i: (i, 0))],
        out_specs=spec,
        out_shape=jax.ShapeDtypeStruct((tok, width), BF),
        compiler_params=params(),
        cost_estimate=cost(4 * tok * tok * width, 8 * tok * width),
        name="query_grad",
    )(g, v, k, state)


def key_value_kernel(head, q_ref, k_ref, v_ref, g_ref, a_ref, ko_ref, vo_ref):
    half = g_ref.shape[0] // 2
    for j in range(g_ref.shape[1] // head):
        at = slice(j * head, (j + 1) * head)
        q, k, v, g, adj = q_ref[:, at], k_ref[:, at], v_ref[:, at], g_ref[:, at], a_ref[at, :]
        first, second = causal_apply(v, g, q, True)
        carried = dot(v, adj, 1, 1)
        ko_ref[:half, at] = (first + carried[:half]).astype(BF)
        ko_ref[half:, at] = (second + carried[half:]).astype(BF)
        first, second = causal_apply(k, q, g, True)
        carried = dot(k, adj, 1, 0)
        vo_ref[:half, at] = (first + carried[:half]).astype(BF)
        vo_ref[half:, at] = (second + carried[half:]).astype(BF)


def key_value_grad_of(q, k, v, g, adjoint, head):
    tok, width = g.shape
    step = 2 * head
    spec = pl.BlockSpec((tok, step), lambda i: (0, i))
    shape = jax.ShapeDtypeStruct((tok, width), BF)
    return pl.pallas_call(
        functools.partial(key_value_kernel, head),
        grid=(width // step,),
        in_specs=[spec, spec, spec, spec, pl.BlockSpec((step, head), lambda i: (i, 0))],
        out_specs=[spec, spec],
        out_shape=[shape, shape],
        compiler_params=params(),
        cost_estimate=cost(8 * tok * tok * width, 12 * tok * width),
        name="key_value_grad",
    )(q, k, v, g, adjoint)


def scan_kernel(n, reverse, x_ref, start_ref, o_ref):
    rows = start_ref.shape[0]
    total = start_ref[...]
    for i in range(n):
        c = n - 1 - i if reverse else i
        at = slice(c * rows, (c + 1) * rows)
        o_ref[at, :] = total.astype(BF)
        total = total + x_ref[at, :].astype(F32)


def scan_blocks(x, start, n, reverse):
    return pl.pallas_call(
        functools.partial(scan_kernel, n, reverse),
        out_shape=jax.ShapeDtypeStruct(x.shape, BF),
        compiler_params=params(),
        cost_estimate=cost(x.size, 4 * x.size),
        name="scan_blocks",
    )(x, start)


def carried(x, start, axis, reverse):
    n = lax.axis_size(axis)
    mine = lax.all_to_all(x, axis, 0, 0, tiled=True)
    return lax.all_to_all(scan_blocks(mine, start, n, reverse), axis, 0, 0, tiled=True)


def local(queries, keys, values, cotangent, out_weight, memory):
    head = memory.shape[2]
    width = queries.shape[1]
    feat = cotangent.shape[1]
    n = lax.axis_size("ctx")
    rows = width // n
    me, tp = lax.axis_index("ctx"), lax.axis_index("tp")

    far = lax.ppermute(cotangent, "tp", [(0, 1), (1, 0)])
    kv = block_sums(keys, values, head)
    start = lax.dynamic_slice_in_dim(memory.reshape(width, head), me * rows, rows, 0)
    state = carried(kv, start, "ctx", False)
    inner = intra(queries, keys, values, head)
    grad, qd = out_grad_and_sums(tp.reshape(1), cotangent, far, out_weight, queries, head)
    adjoint = carried(qd, jnp.zeros_like(start), "ctx", True)
    attended = attended_of(queries, state, inner, head)
    term = weight_term(attended, cotangent, far)
    total = lax.psum_scatter(term, "ctx", scatter_dimension=0, tiled=True)
    query_g = query_grad_of(grad, values, keys, state, head)
    key_g, value_g = key_value_grad_of(queries, keys, values, grad, adjoint, head)
    total = total.astype(F32)
    total = jnp.where(tp == 0, total, jnp.concatenate([total[:, feat:], total[:, :feat]], 1))
    return query_g, key_g, value_g, total


def solution(mesh):
    in_specs = (
        P("ctx", "tp"),
        P("ctx", "tp"),
        P("ctx", "tp"),
        P("ctx", "tp"),
        P("tp", None),
        P("tp", None, None),
    )
    out_specs = (P("ctx", "tp"), P("ctx", "tp"), P("ctx", "tp"), P(("tp", "ctx"), None))
    return jax.shard_map(local, mesh=mesh, in_specs=in_specs, out_specs=out_specs, check_vma=False)
```

time: 492 us -> 203 us (0.41)
  waiting for transfers between devices: 316 us -> 70.4 us
  matrix products: 82 us -> 0 us
  Pallas kernels: 0 us -> 75 us
  other arithmetic: 54.7 us -> 1.08 us
  blocking collectives: 0 us -> 18.7 us
  local copies, waits for them, and re-layouts: 22.7 us -> 4.86 us
  starting transfers between devices: 0.16 us -> 17.1 us
    all_gather x3 -> x0, waiting for transfers between devices: 187 us -> none  [the longest x2 158 us: carried_in(): everything = lax.all_gather(value, axis)]
    reduce_scatter x1, waiting for transfers between devices: 128 us -> 40.9 us  [local(): total = lax.psum_scatter(term, 'ctx', scatter_dimension=0, tiled=True)]
    dot_general x14 -> x0, matrix products: 82 us -> none  [the longest x1 12.5 us: local(): lax.dot_general(attended, full_cot, (((0,), (0,)), ((), ())), preferred_e...]
    pallas_call x0 -> x9, Pallas kernels: none -> 75 us  [the longest x1 14.1 us: key_value_grad_of(): pl.pallas_call(functools.partial(key_value_kernel, head), grid=(width //...]
    select_n x32 -> x1, other arithmetic: 53.3 us -> 1.08 us  [local(): jnp.where(tp == 0, total, jnp.concatenate([total[:, feat:], total[:, :fea...]
    all_to_all x0 -> x3, waiting for transfers between devices: none -> 29.4 us  [the longest x2 17.2 us: carried(): lax.all_to_all(scan_blocks(mine, start, n, reverse), axis, 0, 0, tiled=True)]
    all_to_all x0 -> x1, blocking collectives: none -> 18.7 us  [carried(): mine = lax.all_to_all(x, axis, 0, 0, tiled=True)]
    all_to_all x0 -> x3, starting transfers between devices: none -> 15.5 us  [the longest x2 8.1 us: carried(): lax.all_to_all(scan_blocks(mine, start, n, reverse), axis, 0, 0, tiled=True)]
  transfers between devices with their start and end apart: 4 -> 5, of which waited for: 4 -> 4; matrix products, arithmetic and copies ran while one was open for 32% -> 1% of each run, Pallas kernels for 0% -> 29%
where the time goes in v1:
time: 203 us; the launch traced here: 201 us
  Pallas kernels  75 us (37%)
  waiting for transfers between devices  70.4 us (35%)
  blocking collectives  18.7 us (9%)
  starting transfers between devices  17.1 us (8%)
  between operations  14.1 us (7%)
  local copies, waits for them, and re-layouts  4.86 us (2%)
    reduce_scatter x1, waiting for transfers between devices, local(): total = lax.psum_scatter(term, 'ctx', scatter_dimension=0, tiled=True)  40.9 us
    all_to_all x1, blocking collectives, carried(): mine = lax.all_to_all(x, axis, 0, 0, tiled=True)  18.7 us
    all_to_all x2, waiting for transfers between devices, carried(): lax.all_to_all(scan_blocks(mine, start, n, reverse), axis, 0, 0, tiled=True)  17.2 us
    pallas_call x1, Pallas kernels, key_value_grad_of(): pl.pallas_call(functools.partial(key_value_kernel, head), grid=(width //...  14.1 us
    pallas_call x1, Pallas kernels, out_grad_and_sums(): pl.pallas_call(functools.partial(grad_kernel, head), grid_spec=pltpu.Pref...  12.5 us
    all_to_all x1, waiting for transfers between devices, carried(): mine = lax.all_to_all(x, axis, 0, 0, tiled=True)  12.3 us
    pallas_call x1, Pallas kernels, intra(): pl.pallas_call(functools.partial(intra_kernel, head), grid=(width // step...  10.5 us
    pallas_call x1, Pallas kernels, weight_term(): pl.pallas_call(weight_kernel, grid=(width // step,), in_specs=[pl.BlockSp...  10.2 us
  transfers between devices with their start and end apart: 5, of which 4 were waited for; matrix products, arithmetic and copies ran while one was open for 1% of the time, Pallas kernels for 29%

profile of v1, /device:TPU:0, one launch (start us, length us, event | category | flops | bytes accessed | tf_op | source)
XLA Modules:
  0.0 201.2 jit_solution(3847976554288563872)
XLA Ops:
  7.2 0.0 copy-start
  7.2 0.0 copy-start.4
  7.2 6.8 %block_sums.1 = bf16[2048,128]{1,0:T(8,128)(2,1)} custom-call(bf16[512,2048]{1,0:T(8,128)(2,1)} %k_ref.5, bf16[512,2048]{1,0:T(8,128)(2,1)} %v_ref.5), custom_call_target="tpu_custom_call" | custom-call | flops 268435456 | bytes 4194304 | tf_op jit(solution)/shard_map/block_sums/pallas_call | solution.py:36
  14.0 7.4 %all-to-all-start = ((bf16[16,128,128]{2,1,0:T(8,128)(2,1)}), bf16[16,128,128]{2,1,0:T(8,128)(2,1)S(1)}, u32[]{:S(2)}, u32[]{:S(2)}) async-start(bf16[16,128,128]{2,1,0:T(8,128)(2,1)} %bitcast.13), calls=%async_computation | async-start | bytes 1048576 | tf_op jit(solution)/shard_map/all_to_all | solution.py:268
  21.4 0.0 copy-done.4
  21.4 1.6 collective-permute-start
  23.0 0.0 copy-done
  23.0 0.6 constant_dynamic-slice_fusion.start_ref
  23.6 12.3 %all-to-all-done = bf16[16,128,128]{2,1,0:T(8,128)(2,1)S(1)} async-done(((bf16[16,128,128]{2,1,0:T(8,128)(2,1)}), bf16[16,128,128]{2,1,0:T(8,128)(2,1)S(1)}, u32[]{:S(2)}, u32[]{:S(2)}) %all-to-all-start) | async-done | bytes 524320 | tf_op jit(solution)/shard_map/all_to_all | solution.py:268
  35.9 0.0 copy-start.3
  35.9 0.8 copy-done.3
  36.7 1.9 scan_blocks.2
  38.6 4.1 %all-to-all-start.1 = ((bf16[16,128,128]{2,1,0:T(8,128)(2,1)}), bf16[16,128,128]{2,1,0:T(8,128)(2,1)S(1)}, u32[]{:S(2)}, u32[]{:S(2)}) async-start(bf16[16,128,128]{2,1,0:T(8,128)(2,1)} %bitcast.16), calls=%async_computation.1 | async-start | bytes 1048576 | tf_op jit(solution)/shard_map/all_to_all | solution.py:269
  42.7 0.0 reduce-scatter.2.cloned.1.call-start
  42.7 10.5 %intra.1.i_ref = f32[512,2048]{1,0:T(8,128)} custom-call(bf16[512,2048]{1,0:T(8,128)(2,1)} %q_ref.7, bf16[512,2048]{1,0:T(8,128)(2,1)} %k_ref.5, bf16[512,2048]{1,0:T(8,128)(2,1)} %v_ref.5), custom_call_target="tpu_custom_call" | custom-call | flops 2147483648 | bytes 10485760 | tf_op jit(solution)/shard_map/intra/pallas_call | solution.py:88
  53.3 3.9 %all-to-all-done.1 = bf16[16,128,128]{2,1,0:T(8,128)(2,1)S(1)} async-done(((bf16[16,128,128]{2,1,0:T(8,128)(2,1)}), bf16[16,128,128]{2,1,0:T(8,128)(2,1)S(1)}, u32[]{:S(2)}, u32[]{:S(2)}) %all-to-all-start.1) | async-done | bytes 524320 | tf_op jit(solution)/shard_map/all_to_all | solution.py:269
  57.2 0.0 copy-start.1
  57.2 0.8 copy-done.1
  58.0 7.3 %attended.1.a_ref = bf16[512,2048]{1,0:T(8,128)(2,1)} custom-call(bf16[512,2048]{1,0:T(8,128)(2,1)} %q_ref.7, bf16[2048,128]{1,0:T(8,128)(2,1)} %bitcast.11, f32[512,2048]{1,0:T(8,128)} %intra.1.i_ref), custom_call_target="tpu_custom_call" | custom-call | flops 268435456 | bytes 8388608 | tf_op jit(solution)/shard_map/attended/pallas_call | solution.py:151
  65.2 0.0 collective-permute-done.far_ref
  65.3 10.2 %weight_term.1 = bf16[2048,2048]{1,0:T(8,128)(2,1)} custom-call(bf16[512,2048]{1,0:T(8,128)(2,1)} %attended.1.a_ref, bf16[512,1024]{1,0:T(8,128)(2,1)} %own_ref.3, bf16[512,1024]{1,0:T(8,128)(2,1)} %collective-permute-done.far_ref), custom_call_target="tpu_custom_call" | custom-call | flops 4294967296 | bytes 10485760 | tf_op jit(solution)/shard_map/weight_term/pallas_call | solution.py:175
  75.4 0.0 reduce-scatter.2.cloned.1.call-update
  75.4 12.5 %out_grad.1 = (bf16[512,2048]{1,0:T(8,128)(2,1)}, bf16[2048,128]{1,0:T(8,128)(2,1)}) custom-call(s32[1]{0:T(128)} %bitcast.tp_ref, bf16[512,1024]{1,0:T(8,128)(2,1)} %own_ref.3, bf16[512,1024]{1,0:T(8,128)(2,1)} %collective-permute-done.far_ref, bf16[2048,2048]{1,0:T(8,128)(2,1)} %wf_ref.1, bf16[2048,2048]{1,0:T(8,128)(2,1)} %wf_ref.1, bf16[512,2048]{1,0:T(8,128)(2,1)} %q_ref.7), custom_call_target="tpu_custom_call" | custom-call | flops 4294967296 | bytes 12582912 | tf_op jit(solution)/shard_map/out_grad/pallas_call | solution.py:114
  87.9 18.7 %all_to_all.44 = bf16[16,128,128]{2,1,0:T(8,128)(2,1)} all-to-all(bf16[16,128,128]{2,1,0:T(8,128)(2,1)} %bitcast.19), channel_id=1, replica_groups=mesh['ctx'=16,'tp'=2] {'ctx'}, dimensions={0} | all-to-all | bytes 1048576 | tf_op jit(solution)/shard_map/all_to_all | solution.py:268
  106.6 0.6 broadcast_in_dim.3.start_ref
  107.3 1.9 scan_blocks.3
  109.2 4.0 %all-to-all-start.3 = ((bf16[16,128,128]{2,1,0:T(8,128)(2,1)}), bf16[16,128,128]{2,1,0:T(8,128)(2,1)S(1)}, u32[]{:S(2)}, u32[]{:S(2)}) async-start(bf16[16,128,128]{2,1,0:T(8,128)(2,1)} %bitcast.15), calls=%async_computation.3 | async-start | bytes 1048576 | tf_op jit(solution)/shard_map/all_to_all | solution.py:269
  113.2 9.8 %query_grad.1 = bf16[512,2048]{1,0:T(8,128)(2,1)} custom-call(bf16[512,2048]{1,0:T(8,128)(2,1)} %get-tuple-element.8.g_ref, bf16[512,2048]{1,0:T(8,128)(2,1)} %v_ref.5, bf16[512,2048]{1,0:T(8,128)(2,1)} %k_ref.5, bf16[2048,128]{1,0:T(8,128)(2,1)} %bitcast.12), custom_call_target="tpu_custom_call" | custom-call | flops 2147483648 | bytes 8388608 | tf_op jit(solution)/shard_map/query_grad/pallas_call | solution.py:202
  123.0 13.3 %all-to-all-done.3 = bf16[16,128,128]{2,1,0:T(8,128)(2,1)S(1)} async-done(((bf16[16,128,128]{2,1,0:T(8,128)(2,1)}), bf16[16,128,128]{2,1,0:T(8,128)(2,1)S(1)}, u32[]{:S(2)}, u32[]{:S(2)}) %all-to-all-start.3) | async-done | bytes 524320 | tf_op jit(solution)/shard_map/all_to_all | solution.py:269
  136.3 0.0 copy-start.5
  136.3 0.8 copy-done.5
  137.1 14.1 %key_value_grad.1 = (bf16[512,2048]{1,0:T(8,128)(2,1)}, bf16[512,2048]{1,0:T(8,128)(2,1)}) custom-call(bf16[512,2048]{1,0:T(8,128)(2,1)} %q_ref.7, bf16[512,2048]{1,0:T(8,128)(2,1)} %k_ref.5, bf16[512,2048]{1,0:T(8,128)(2,1)} %v_ref.5, bf16[512,2048]{1,0:T(8,128)(2,1)} %get-tuple-element.8.g_ref, bf16[2048,128]{1,0:T(8,128)(2,1)} %bitcast.18), custom_call_target="tpu_custom_call" | custom-call | flops 4294967296 | bytes 12582912 | tf_op jit(solution)/shard_map/key_value_grad/pallas_call | solution.py:234
  151.2 40.9 %reduce-scatter.2.cloned.1.call-done = bf16[128,2048]{1,0:T(8,128)(2,1)} async-done(((bf16[2048,2048]{1,0:T(8,128)(2,1)}), bf16[128,2048]{1,0:T(8,128)(2,1)}) %reduce-scatter.2.cloned.1.call-update) | async-done | bytes 524304 | tf_op jit(solution)/shard_map/reduce_scatter | solution.py:289
  192.1 0.0 copy-start.2
  192.1 1.2 fusion
  193.3 0.0 copy-done.2
  193.3 1.1 maximum_select_fusion
Async XLA Ops:
  7.2 15.8 %copy-start = (f32[16,128,128]{2,1,0:T(8,128)S(1)}, f32[16,128,128]{2,1,0:T(8,128)}, u32[]{:S(2)}) copy-start(f32[16,128,128]{2,1,0:T(8,128)} %param.11) | copy-start | bytes 3145732
  7.2 14.2 %copy-start.4 = (bf16[512,1024]{1,0:T(8,128)(2,1)S(1)}, bf16[512,1024]{1,0:T(8,128)(2,1)}, u32[]{:S(2)}) copy-start(bf16[512,1024]{1,0:T(8,128)(2,1)} %own_ref.3) | copy-start | bytes 3145732
  14.0 21.9 %all-to-all-start = ((bf16[16,128,128]{2,1,0:T(8,128)(2,1)}), bf16[16,128,128]{2,1,0:T(8,128)(2,1)S(1)}, u32[]{:S(2)}, u32[]{:S(2)}) async-start(bf16[16,128,128]{2,1,0:T(8,128)(2,1)} %bitcast.13), calls=%async_computation | async-start | bytes 1048576 | tf_op jit(solution)/shard_map/all_to_all | solution.py:268
  21.4 43.8 %collective-permute-start = (bf16[512,1024]{1,0:T(8,128)(2,1)S(1)}, bf16[512,1024]{1,0:T(8,128)(2,1)}, u32[]{:S(2)}, u32[]{:S(2)}) collective-permute-start(bf16[512,1024]{1,0:T(8,128)(2,1)S(1)} %copy-done.4), channel_id=1, source_target_pairs={{0,1},{1,0},{2,3},{3,2},{4,5},{5,4},{6,7},{7,6},{8,9},{9,8},{10,11... | collective-permute-start | bytes 3145736 | tf_op jit(solution)/shard_map/ppermute | solution.py:280
  35.9 0.8 copy-start.3
  38.6 18.6 %all-to-all-start.1 = ((bf16[16,128,128]{2,1,0:T(8,128)(2,1)}), bf16[16,128,128]{2,1,0:T(8,128)(2,1)S(1)}, u32[]{:S(2)}, u32[]{:S(2)}) async-start(bf16[16,128,128]{2,1,0:T(8,128)(2,1)} %bitcast.16), calls=%async_computation.1 | async-start | bytes 1048576 | tf_op jit(solution)/shard_map/all_to_all | solution.py:269
  42.7 149.4 %reduce-scatter.2.cloned.1.call-start = ((), (), s32[]{:S(2)}) async-start(), calls=%async_computation.5 | async-start | bytes 8912896 | tf_op jit(solution)/shard_map/reduce_scatter | solution.py:289
  57.2 0.8 copy-start.1
  109.2 27.1 %all-to-all-start.3 = ((bf16[16,128,128]{2,1,0:T(8,128)(2,1)}), bf16[16,128,128]{2,1,0:T(8,128)(2,1)S(1)}, u32[]{:S(2)}, u32[]{:S(2)}) async-start(bf16[16,128,128]{2,1,0:T(8,128)(2,1)} %bitcast.15), calls=%async_computation.3 | async-start | bytes 1048576 | tf_op jit(solution)/shard_map/all_to_all | solution.py:269
  136.3 0.8 copy-start.5
  192.1 1.2 copy-start.2
Sparse Core Ops, SparseCore 0:
  75.6 116.4 reduce-scatter.1

commit v2 on v1

--- a/solution.py
+++ b/solution.py
@@ -269,7 +269,254 @@
     return lax.all_to_all(scan_blocks(mine, start, n, reverse), axis, 0, 0, tiled=True)
 
 
-def local(queries, keys, values, cotangent, out_weight, memory):
+def pair_sums_kernel(head, me_ref, a_ref, b_ref, mine_ref, send_ref):
+    even = dot(a_ref[:, :head], b_ref[:, :head], 0, 0)
+    odd = dot(a_ref[:, head:], b_ref[:, head:], 0, 0)
+    first = me_ref[0] % 2 == 0
+    mine_ref[...] = jnp.where(first, even, odd).astype(BF)
+    send_ref[...] = jnp.where(first, odd, even).astype(BF)
+
+
+def pair_sums(me, a, b, head):
+    tok, width = a.shape
+    spec = pl.BlockSpec((tok, 2 * head), lambda i, m: (0, i))
+    out = pl.BlockSpec((head, head), lambda i, m: (i, 0))
+    shape = jax.ShapeDtypeStruct((width // 2, head), BF)
+    return pl.pallas_call(
+        functools.partial(pair_sums_kernel, head),
+        grid_spec=pltpu.PrefetchScalarGridSpec(
+            num_scalar_prefetch=1,
+            grid=(width // (2 * head),),
+            in_specs=[spec] * 2,
+            out_specs=[out] * 2,
+        ),
+        out_shape=[shape] * 2,
+        compiler_params=params(),
+        cost_estimate=cost(2 * tok * width * head, 4 * tok * width),
+        name="pair_sums",
+    )(me, a, b)
+
+
+def pair_intra_kernel(head, me_ref, q_ref, k_ref, v_ref, mine_ref, send_ref):
+    first = me_ref[0] % 2 == 0
+    half = q_ref.shape[0] // 2
+    even, odd = slice(0, head), slice(head, 2 * head)
+    parts = [causal_apply(q_ref[:, at], k_ref[:, at], v_ref[:, at], False) for at in (even, odd)]
+    for k, at in enumerate((slice(0, half), slice(half, 2 * half))):
+        mine_ref[at, :] = jnp.where(first, parts[0][k], parts[1][k]).astype(BF)
+        send_ref[at, odd] = jnp.where(first, parts[1][k], parts[0][k]).astype(BF)
+    send_ref[:, even] = jnp.where(first, q_ref[:, odd], q_ref[:, even])
+
+
+def pair_intra(me, q, k, v, head):
+    tok, width = q.shape
+    spec = pl.BlockSpec((tok, 2 * head), lambda i, m: (0, i))
+    return pl.pallas_call(
+        functools.partial(pair_intra_kernel, head),
+        grid_spec=pltpu.PrefetchScalarGridSpec(
+            num_scalar_prefetch=1,
+            grid=(width // (2 * head),),
+            in_specs=[spec] * 3,
+            out_specs=[pl.BlockSpec((tok, head), lambda i, m: (0, i)), spec],
+        ),
+        out_shape=[
+            jax.ShapeDtypeStruct((tok, width // 2), BF),
+            jax.ShapeDtypeStruct((tok, width), BF),
+        ],
+        compiler_params=params(),
+        cost_estimate=cost(4 * tok * tok * width, 9 * tok * width),
+        name="pair_intra",
+    )(me, q, k, v)
+
+
+def pair_attended_kernel(head, me_ref, q0_ref, q1_ref, i_ref, far_ref, s_ref, own_ref, oth_ref,
+                         mine_ref, send_ref, so_ref, sf_ref):
+    core = (me_ref[0] % 2).astype(F32)
+    south = (me_ref[0] // 2) % 2 == 0
+    state = s_ref[...].astype(F32)
+    near = (state + core * oth_ref[...].astype(F32)).astype(BF)
+    away = (state + (1.0 - core) * own_ref[...].astype(F32)).astype(BF)
+    so_ref[...] = near
+    sf_ref[...] = away
+    results = []
+    for j, q_ref in enumerate((q0_ref, q1_ref)):
+        at = slice(j * head, (j + 1) * head)
+        here = dot(q_ref[...], near[at], 1, 0) + i_ref[:, at].astype(F32)
+        base = 2 * j * head
+        q_far = far_ref[:, base : base + head]
+        there = dot(q_far, away[at], 1, 0) + far_ref[:, base + head : base + 2 * head].astype(F32)
+        results.append((here, there))
+    for k in range(2):
+        mine_ref[k] = jnp.where(south, results[0][k], results[1][k]).astype(BF)
+        send_ref[k] = jnp.where(south, results[1][k], results[0][k]).astype(BF)
+
+
+def pair_attended(me, q, inner, far, state, own, oth, head):
+    tok, width = q.shape
+    steps = width // (4 * head)
+    rows = pl.BlockSpec((2 * head, head), lambda i, m: (i, 0))
+    out = pl.BlockSpec((2, tok, head), lambda i, m: (0, 0, i))
+    return pl.pallas_call(
+        functools.partial(pair_attended_kernel, head),
+        grid_spec=pltpu.PrefetchScalarGridSpec(
+            num_scalar_prefetch=1,
+            grid=(steps,),
+            in_specs=[
+                pl.BlockSpec((tok, head), lambda i, m: (0, 4 * i + m[0] % 2)),
+                pl.BlockSpec((tok, head), lambda i, m: (0, 4 * i + 2 + m[0] % 2)),
+                pl.BlockSpec((tok, 2 * head), lambda i, m: (0, i)),
+                pl.BlockSpec((tok, 4 * head), lambda i, m: (0, i)),
+                rows,
+                rows,
+                rows,
+            ],
+            out_specs=[out, out, rows, rows],
+        ),
+        out_shape=[
+            jax.ShapeDtypeStruct((2, tok, width // 4), BF),
+            jax.ShapeDtypeStruct((2, tok, width // 4), BF),
+            jax.ShapeDtypeStruct((width // 2, head), BF),
+            jax.ShapeDtypeStruct((width // 2, head), BF),
+        ],
+        compiler_params=params(),
+        cost_estimate=cost(2 * tok * head * width, 8 * tok * width),
+        name="pair_attended",
+    )(me, q, q, inner, far, state, own, oth)
+
+
+def quad_weight_kernel(a_ref, b_ref, *refs):
+    ins, (o_ref, at_ref) = refs[:8], refs[8:]
+    tok = a_ref.shape[1]
+
+    @pl.when(pl.program_id(0) == 0)
+    def _():
+        for k in range(4):
+            block = (a_ref if k < 2 else b_ref)[k % 2]
+            at_ref[:, k * tok : (k + 1) * tok] = block.T
+
+    for part in range(2):
+        total = None
+        for k in range(4):
+            term = dot(at_ref[:, k * tok : (k + 1) * tok], ins[2 * k + part][...], 1, 0)
+            total = term if total is None else total + term
+        o_ref[part] = total.astype(BF)
+
+
+def quad_weight(a, b, cots):
+    _, tok, cols = a.shape
+    feat = cots[0].shape[1]
+    step = min(256, feat)
+    whole = pl.BlockSpec(a.shape, lambda i: (0, 0, 0))
+    return pl.pallas_call(
+        quad_weight_kernel,
+        grid=(feat // step,),
+        in_specs=[whole, whole] + [pl.BlockSpec((tok, step), lambda i: (0, i))] * 8,
+        out_specs=pl.BlockSpec((2, cols, step), lambda i: (0, 0, i)),
+        out_shape=jax.ShapeDtypeStruct((2, cols, feat), BF),
+        scratch_shapes=[pltpu.VMEM((cols, 4 * tok), BF)],
+        compiler_params=params(),
+        cost_estimate=cost(16 * tok * feat * cols, 20 * feat * tok),
+        name="quad_weight",
+    )(a, b, *cots)
+
+
+def pair_query_kernel(head, me_ref, g_ref, v_ref, k_ref, s_ref, t_ref, o_ref):
+    first = me_ref[0] % 2 == 0
+    half = g_ref.shape[0] // 2
+    for j in range(2):
+        at = slice(j * head, (j + 1) * head)
+        g = g_ref[:, at]
+        state = jnp.where(first == (j == 0), s_ref[...], t_ref[...])
+        first_half, second_half = causal_apply(g, v_ref[:, at], k_ref[:, at], False)
+        over = dot(g, state, 1, 1)
+        o_ref[:half, at] = (first_half + over[:half]).astype(BF)
+        o_ref[half:, at] = (second_half + over[half:]).astype(BF)
+
+
+def pair_query_grad(me, g, v, k, mine, other, head):
+    tok, width = g.shape
+    spec = pl.BlockSpec((tok, 2 * head), lambda i, m: (0, i))
+    rows = pl.BlockSpec((head, head), lambda i, m: (i, 0))
+    return pl.pallas_call(
+        functools.partial(pair_query_kernel, head),
+        grid_spec=pltpu.PrefetchScalarGridSpec(
+            num_scalar_prefetch=1,
+            grid=(width // (2 * head),),
+            in_specs=[spec, spec, spec, rows, rows],
+            out_specs=spec,
+        ),
+        out_shape=jax.ShapeDtypeStruct((tok, width), BF),
+        compiler_params=params(),
+        cost_estimate=cost(4 * tok * tok * width, 8 * tok * width),
+        name="query_grad",
+    )(me, g, v, k, mine, other)
+
+
+def line_reduce(term, line, n):
+    places = n // 4
+    right = left = None
+    for r in range(1, places):
+        to_right = lax.dynamic_index_in_dim(term, jnp.minimum(line + places - r, places - 1), 1, False)
+        to_left = lax.dynamic_index_in_dim(term, jnp.maximum(line - places + r, 0), 1, False)
+        if right is not None:
+            to_right = (to_right.astype(F32) + right.astype(F32)).astype(BF)
+            to_left = (to_left.astype(F32) + left.astype(F32)).astype(BF)
+        right = lax.ppermute(to_right, "ctx", [(c, c + 4) for c in range(n) if c // 4 < r])
+        left = lax.ppermute(to_left, "ctx", [(c, c - 4) for c in range(n) if c // 4 >= places - r])
+    total = lax.dynamic_index_in_dim(term, line, 1, False).astype(F32)
+    if right is not None:
+        total = total + right.astype(F32) + left.astype(F32)
+    return total
+
+
+def local_paired(queries, keys, values, cotangent, out_weight, memory):
+    head = memory.shape[2]
+    tok, width = queries.shape
+    n = lax.axis_size("ctx")
+    me, tp = lax.axis_index("ctx"), lax.axis_index("tp")
+    who = me.reshape(1)
+
+    def swap(x, bit):
+        return lax.ppermute(x, "ctx", [(c, c ^ bit) for c in range(n)])
+
+    def swap_tp(x):
+        return lax.ppermute(x, "tp", [(0, 1), (1, 0)])
+
+    kv_mine, kv_send = pair_sums(who, keys, values, head)
+    kv_other = swap(kv_send, 1)
+    groups = [[c for c in range(n) if c % 2 == core] for core in range(2)]
+    chip = (kv_mine.astype(F32) + kv_other.astype(F32)).astype(BF)
+    chip = lax.all_to_all(chip, "ctx", 0, 0, axis_index_groups=groups, tiled=True)
+    start = lax.dynamic_index_in_dim(memory, me, 0, False)
+    chip = scan_blocks(chip, start, n // 2, False)
+    state = lax.all_to_all(chip, "ctx", 0, 0, axis_index_groups=groups, tiled=True)
+
+    far = swap_tp(cotangent)
+    south = swap(cotangent, 2)
+    far_south = swap_tp(south)
+    cots = [cotangent, far, swap(cotangent, 1), swap(far, 1)]
+    cots += [south, far_south, swap(south, 1), swap(far_south, 1)]
+
+    inner, sent = pair_intra(who, queries, keys, values, head)
+    got = swap(sent, 1)
+    grad, qd = out_grad_and_sums(tp.reshape(1), cotangent, far, out_weight, queries, head)
+
+    mine, send, state_mine, state_send = pair_attended(
+        who, queries, inner, got, state, kv_mine, kv_other, head
+    )
+    received = swap(send, 2)
+    state_other = swap(state_send, 1)
+    adjoint = carried(qd, jnp.zeros_like(start), "ctx", True)
+    term = quad_weight(mine, received, cots)
+    feat = cotangent.shape[1]
+    total = line_reduce(term.reshape(2, n // 4, head, feat), me // 4, n)
+    query_g = pair_query_grad(who, grad, values, keys, state_mine, state_other, head)
+    key_g, value_g = key_value_grad_of(queries, keys, values, grad, adjoint, head)
+    first, second = jnp.where(tp == 0, total[0], total[1]), jnp.where(tp == 0, total[1], total[0])
+    return query_g, key_g, value_g, jnp.concatenate([first, second], 1)
+
+
+def local_any(queries, keys, values, cotangent, out_weight, memory):
     head = memory.shape[2]
     width = queries.shape[1]
     feat = cotangent.shape[1]
@@ -294,6 +541,14 @@
     return query_g, key_g, value_g, total
 
 
+def local(*args):
+    heads = args[5].shape[0]
+    n = lax.axis_size("ctx")
+    if n == heads and n % 4 == 0 and lax.axis_size("tp") == 2:
+        return local_paired(*args)
+    return local_any(*args)
+
+
 def solution(mesh):
     in_specs = (
         P("ctx", "tp"),

time: 203 us -> 183 us (0.901)
  starting transfers between devices: 17.1 us -> 59.5 us
  waiting for transfers between devices: 70.4 us -> 33.6 us
  blocking collectives: 18.7 us -> 0 us
  between operations: 14.1 us -> 0.82 us
  other arithmetic: 1.08 us -> 9.6 us
  Pallas kernels: 75 us -> 71 us
  local copies, waits for them, and re-layouts: 4.86 us -> 7.01 us
    reduce_scatter x1 -> x0, waiting for transfers between devices: 40.9 us -> none  [local(): total = lax.psum_scatter(term, 'ctx', scatter_dimension=0, tiled=True)]
    ppermute x1 -> x17, starting transfers between devices: 1.56 us -> 38.2 us  [the longest x3 26.1 us: line_reduce(): lax.ppermute(to_right, 'ctx', [(c, c + 4) for c in range(n) if c // 4 < r])]
    all_to_all x1 -> x0, blocking collectives: 18.7 us -> none  [carried(): mine = lax.all_to_all(x, axis, 0, 0, tiled=True)]
    ppermute x1 -> x17, waiting for transfers between devices: 0.01 us -> 18.3 us  [the longest x3 9.55 us: line_reduce(): lax.ppermute(to_right, 'ctx', [(c, c + 4) for c in range(n) if c // 4 < r])]
    all_to_all x2 -> x1, waiting for transfers between devices: 17.2 us -> 0.01 us  [carried(): lax.all_to_all(scan_blocks(mine, start, n, reverse), axis, 0, 0, tiled=True)]
    all_to_all x0 -> x2, waiting for transfers between devices: none -> 15.3 us  [local_paired(): lax.all_to_all(chip, 'ctx', 0, 0, axis_index_groups=groups, tiled=True)]
    all_to_all x1, waiting for transfers between devices: 12.3 us -> 0.01 us  [carried(): mine = lax.all_to_all(x, axis, 0, 0, tiled=True)]
    all_to_all x0 -> x2, starting transfers between devices: none -> 9.87 us  [local_paired(): lax.all_to_all(chip, 'ctx', 0, 0, axis_index_groups=groups, tiled=True)]
  transfers between devices with their start and end apart: 5 -> 21, of which waited for: 4 -> 6; matrix products, arithmetic and copies ran while one was open for 1% -> 6% of each run, Pallas kernels for 29% -> 39%
where the time goes in v2:
time: 183 us; the launch traced here: 182 us
  Pallas kernels  71 us (39%)
  starting transfers between devices  59.5 us (33%)
  waiting for transfers between devices  33.6 us (18%)
  other arithmetic  9.6 us (5%)
  local copies, waits for them, and re-layouts  7.01 us (4%)
    ppermute x3, starting transfers between devices, line_reduce(): lax.ppermute(to_right, 'ctx', [(c, c + 4) for c in range(n) if c // 4 < r])  26.1 us
    all_to_all x2, waiting for transfers between devices, local_paired(): lax.all_to_all(chip, 'ctx', 0, 0, axis_index_groups=groups, tiled=True)  15.3 us
    pallas_call x1, Pallas kernels, key_value_grad_of(): pl.pallas_call(functools.partial(key_value_kernel, head), grid=(width //...  14 us
    pallas_call x1, Pallas kernels, out_grad_and_sums(): pl.pallas_call(functools.partial(grad_kernel, head), grid_spec=pltpu.Pref...  12 us
    pallas_call x1, Pallas kernels, pair_intra(): pl.pallas_call(functools.partial(pair_intra_kernel, head), grid_spec=pltp...  10.3 us
    all_to_all x2, starting transfers between devices, local_paired(): lax.all_to_all(chip, 'ctx', 0, 0, axis_index_groups=groups, tiled=True)  9.87 us
    pallas_call x1, Pallas kernels, pair_query_grad(): pl.pallas_call(functools.partial(pair_query_kernel, head), grid_spec=pltp...  9.87 us
    pallas_call x1, Pallas kernels, quad_weight(): pl.pallas_call(quad_weight_kernel, grid=(feat // step,), in_specs=[whole,...  9.56 us
  transfers between devices with their start and end apart: 21, of which 6 were waited for; matrix products, arithmetic and copies ran while one was open for 6% of the time, Pallas kernels for 39%

profile of v2, /device:TPU:0, one launch (start us, length us, event | category | flops | bytes accessed | tf_op | source)
XLA Modules:
  0.0 181.5 jit_solution(8579055284328575984)
XLA Ops:
  0.6 0.0 copy-start
  0.6 3.0 %collective-permute-start.7 = (bf16[512,1024]{1,0:T(8,128)(2,1)}, bf16[512,1024]{1,0:T(8,128)(2,1)}, u32[]{:S(2)}, u32[]{:S(2)}) collective-permute-start(bf16[512,1024]{1,0:T(8,128)(2,1)} %refs_0_.1), channel_id=1, source_target_pairs={{0,4},{2,6},{4,0},{6,2},{8,12},{10,14},{12,8},{14,10},{16,20},{18,... | collective-permute-start | bytes 3145736 | tf_op jit(solution)/shard_map/ppermute | solution.py:480
  3.7 10.3 %pair_intra.1 = (bf16[512,1024]{1,0:T(8,128)(2,1)}, bf16[512,2048]{1,0:T(8,128)(2,1)}) custom-call(s32[1]{0:T(128)} %bitcast.me_ref, bf16[512,2048]{1,0:T(8,128)(2,1)} %q_ref.5, bf16[512,2048]{1,0:T(8,128)(2,1)} %k_ref.5, bf16[512,2048]{1,0:T(8,128)(2,1)} %v_ref.5), custom_call_target="tpu_custom_call" | custom-call | flops 2147483648 | bytes 9437184 | tf_op jit(solution)/shard_map/pair_intra/pallas_call | solution.py:314
  14.0 6.7 %pair_sums.1 = (bf16[1024,128]{1,0:T(8,128)(2,1)}, bf16[1024,128]{1,0:T(8,128)(2,1)}) custom-call(s32[1]{0:T(128)} %bitcast.me_ref, bf16[512,2048]{1,0:T(8,128)(2,1)} %k_ref.5, bf16[512,2048]{1,0:T(8,128)(2,1)} %v_ref.5), custom_call_target="tpu_custom_call" | custom-call | flops 268435456 | bytes 4194304 | tf_op jit(solution)/shard_map/pair_sums/pallas_call | solution.py:285
  20.7 0.5 collective-permute-start.2
  21.2 1.5 collective-permute-start
  22.6 4.5 %collective-permute-done.7.refs_4_ = bf16[512,1024]{1,0:T(8,128)(2,1)} collective-permute-done((bf16[512,1024]{1,0:T(8,128)(2,1)}, bf16[512,1024]{1,0:T(8,128)(2,1)}, u32[]{:S(2)}, u32[]{:S(2)}) %collective-permute-start.7) | collective-permute-done | bytes 1048608 | tf_op jit(solution)/shard_map/ppermute | solution.py:480
  27.2 1.7 collective-permute-start.8
  28.9 1.8 %add_convert_fusion = bf16[1024,128]{1,0:T(8,128)(2,1)} fusion(bf16[1024,128]{1,0:T(8,128)(2,1)S(1)} %collective-permute-done.2.oth_ref, bf16[1024,128]{1,0:T(8,128)(2,1)} %get-tuple-element.19.own_ref), kind=kLoop, calls=%fused_computation.15 | loop fusion | flops 524288 | bytes 786432 | tf_op jit(solution)/shard_map/convert_element_type | solution.py:488
  30.7 5.8 %all-to-all-start = ((bf16[8,128,128]{2,1,0:T(8,128)(2,1)}), bf16[8,128,128]{2,1,0:T(8,128)(2,1)}, u32[]{:S(2)}, u32[]{:S(2)}) async-start(bf16[8,128,128]{2,1,0:T(8,128)(2,1)} %bitcast.51), calls=%async_computation | async-start | bytes 524288 | tf_op jit(solution)/shard_map/all_to_all | solution.py:489
  36.5 0.6 dynamic-slice_bitcast_fusion.2.start_ref
  37.2 7.7 %all-to-all-done = bf16[8,128,128]{2,1,0:T(8,128)(2,1)} async-done(((bf16[8,128,128]{2,1,0:T(8,128)(2,1)}), bf16[8,128,128]{2,1,0:T(8,128)(2,1)}, u32[]{:S(2)}, u32[]{:S(2)}) %all-to-all-start) | async-done | bytes 262176 | tf_op jit(solution)/shard_map/all_to_all | solution.py:489
  44.8 1.7 scan_blocks.2
  46.5 4.0 %all-to-all-start.1 = ((bf16[8,128,128]{2,1,0:T(8,128)(2,1)}), bf16[8,128,128]{2,1,0:T(8,128)(2,1)}, u32[]{:S(2)}, u32[]{:S(2)}) async-start(bf16[8,128,128]{2,1,0:T(8,128)(2,1)} %bitcast.52), calls=%async_computation.1 | async-start | bytes 524288 | tf_op jit(solution)/shard_map/all_to_all | solution.py:492
  50.6 0.1 collective-permute-start.5
  50.7 0.5 collective-permute-start.9
  51.2 0.1 collective-permute-start.6
  51.3 7.6 %all-to-all-done.1 = bf16[8,128,128]{2,1,0:T(8,128)(2,1)} async-done(((bf16[8,128,128]{2,1,0:T(8,128)(2,1)}), bf16[8,128,128]{2,1,0:T(8,128)(2,1)}, u32[]{:S(2)}, u32[]{:S(2)}) %all-to-all-start.1) | async-done | bytes 262176 | tf_op jit(solution)/shard_map/all_to_all | solution.py:492
  58.8 1.3 copy-done.2
  60.2 4.9 %pair_attended.1 = (bf16[2,512,512]{2,1,0:T(8,128)(2,1)}, bf16[2,512,512]{2,1,0:T(8,128)(2,1)}, bf16[1024,128]{1,0:T(8,128)(2,1)}, bf16[1024,128]{1,0:T(8,128)(2,1)}) custom-call(s32[1]{0:T(128)} %bitcast.me_ref, bf16[512,2048]{1,0:T(8,128)(2,1)} %q_ref.5, bf16[512,2048]{1,0:T(8,128)(2,1)} %q_ref.5, bf16[512,1024]{1,0:T(8,128)(2,1)} %get-tuple-element.17.i_ref, ...), custom_call_target="tpu_custom_call" | custom-call | flops 268435456 | bytes 8388608 | tf_op jit(solution)/shard_map/pair_attended/pallas_call | solution.py:359
  65.1 0.1 collective-permute-start.4
  65.2 3.9 %collective-permute-done.8.refs_5_ = bf16[512,1024]{1,0:T(8,128)(2,1)} collective-permute-done((bf16[512,1024]{1,0:T(8,128)(2,1)}, bf16[512,1024]{1,0:T(8,128)(2,1)}, u32[]{:S(2)}, u32[]{:S(2)}) %collective-permute-start.8) | collective-permute-done | bytes 1048608 | tf_op jit(solution)/shard_map/ppermute | solution.py:483
  69.1 12.0 %out_grad.1 = (bf16[512,2048]{1,0:T(8,128)(2,1)}, bf16[2048,128]{1,0:T(8,128)(2,1)}) custom-call(s32[1]{0:T(128)} %bitcast.1.tp_ref, bf16[512,1024]{1,0:T(8,128)(2,1)} %refs_0_.1, bf16[512,1024]{1,0:T(8,128)(2,1)} %collective-permute-done.far_ref.refs_1_, bf16[2048,2048]{1,0:T(8,128)(2,1)} %wf_ref.1, bf16[2048,2048]{1,0:T(8,128)(2,1)} %wf_ref.1, ...), custom_call_target="tpu_custom_call" | custom-call | flops 4294967296 | bytes 12582912 | tf_op jit(solution)/shard_map/out_grad/pallas_call | solution.py:114
  81.1 5.1 %all-to-all-start.2 = ((bf16[16,128,128]{2,1,0:T(8,128)(2,1)}), bf16[16,128,128]{2,1,0:T(8,128)(2,1)}, u32[]{:S(2)}, u32[]{:S(2)}) async-start(bf16[16,128,128]{2,1,0:T(8,128)(2,1)} %bitcast.53), calls=%async_computation.2 | async-start | bytes 1048576 | tf_op jit(solution)/shard_map/all_to_all | solution.py:268
  86.3 0.3 collective-permute-done.4.b_ref
  86.6 1.0 copy-done.5
  87.6 0.3 copy-done.6
  87.9 9.6 %quad_weight.1 = bf16[2,512,1024]{2,1,0:T(8,128)(2,1)} custom-call(bf16[2,512,512]{2,1,0:T(8,128)(2,1)} %get-tuple-element.26.a_ref, bf16[2,512,512]{2,1,0:T(8,128)(2,1)} %copy-done.5, bf16[512,1024]{1,0:T(8,128)(2,1)} %refs_0_.1, bf16[512,1024]{1,0:T(8,128)(2,1)} %collective-permute-done.far_ref.refs_1_, bf16[512,1024]{1,0:T(8,128)(2,1)} %collective-permute-done.5.refs_2_, ...), custom_call_target="tpu_custom_call" | custom-call | flops 4294967296 | bytes 10485760 | tf_op jit(solution)/shard_map/quad_weight/pallas_call | solution.py:410
  97.5 2.4 %dynamic-slice_bitcast_fusion.1 = (bf16[2,128,1024]{2,1,0:T(8,128)(2,1)}, bf16[2,128,1024]{2,1,0:T(8,128)(2,1)}) fusion(bf16[2,4,128,1024]{3,2,1,0:T(8,128)(2,1)} %bitcast.46, s32[]{:T(128)S(6)} %select_n.49, s32[]{:T(128)S(6)} %max.11), kind=kLoop, calls=%fused_computation.14 | loop fusion | bytes 2097160 | tf_op jit(solution)/shard_map/jit(dynamic_index_in_dim)/squeeze | solution.py:459
  99.8 4.3 %collective-permute-start.11 = (bf16[2,128,1024]{2,1,0:T(8,128)(2,1)}, bf16[2,128,1024]{2,1,0:T(8,128)(2,1)}, u32[]{:S(2)}, u32[]{:S(2)}) collective-permute-start(bf16[2,128,1024]{2,1,0:T(8,128)(2,1)} %get-tuple-element.32), channel_id=1, source_target_pairs={{0,8},{2,10},{4,12},{6,14},{1,9},{3,11},{5,13},{7,15}} | collective-permute-start | bytes 1572872 | tf_op jit(solution)/shard_map/ppermute | solution.py:464
  104.1 1.5 collective-permute-start.14
  105.6 9.5 %collective-permute-done.11 = bf16[2,128,1024]{2,1,0:T(8,128)(2,1)} collective-permute-done((bf16[2,128,1024]{2,1,0:T(8,128)(2,1)}, bf16[2,128,1024]{2,1,0:T(8,128)(2,1)}, u32[]{:S(2)}, u32[]{:S(2)}) %collective-permute-start.11) | collective-permute-done | bytes 524320 | tf_op jit(solution)/shard_map/ppermute | solution.py:464
  115.1 2.6 %fusion.2 = (bf16[2,128,1024]{2,1,0:T(8,128)(2,1)}, bf16[2,128,1024]{2,1,0:T(8,128)(2,1)}) fusion(bf16[2,128,1024]{2,1,0:T(8,128)(2,1)} %collective-permute-done.11, bf16[2,4,128,1024]{3,2,1,0:T(8,128)(2,1)S(1)} %bitcast.47, s32[]{:T(128)S(6)} %select_n.48, bf16[2,128,1024]{2,1,0:T(8,128)(2,1)} %collective-permute-done.14, s32[]{:T(128)S(6)} %max.10), kind=kLoop, calls=%fused_computation.6 | loop fusion | flops 2097152 | bytes 3145736 | tf_op jit(solution)/shard_map/convert_element_type | solution.py:462
  117.7 5.2 %collective-permute-start.12 = (bf16[2,128,1024]{2,1,0:T(8,128)(2,1)}, bf16[2,128,1024]{2,1,0:T(8,128)(2,1)}, u32[]{:S(2)}, u32[]{:S(2)}) collective-permute-start(bf16[2,128,1024]{2,1,0:T(8,128)(2,1)} %get-tuple-element.30), channel_id=1, source_target_pairs={{0,8},{2,10},{4,12},{6,14},{8,16},{10,18},{12,20},{14,22},{1,9},{3... | collective-permute-start | bytes 1572872 | tf_op jit(solution)/shard_map/ppermute | solution.py:464
  122.9 1.5 collective-permute-start.15
  124.3 0.6 broadcast_in_dim.3.start_ref
  125.0 1.9 %scan_blocks.3 = bf16[2048,128]{1,0:T(8,128)(2,1)} custom-call(bf16[2048,128]{1,0:T(8,128)(2,1)} %bitcast.8.x_ref, f32[128,128]{1,0:T(8,128)} %broadcast_in_dim.3.start_ref), custom_call_target="tpu_custom_call" | custom-call | flops 262144 | bytes 1048576 | tf_op jit(solution)/shard_map/scan_blocks/pallas_call | solution.py:257
  126.9 6.4 %all-to-all-start.3 = ((bf16[16,128,128]{2,1,0:T(8,128)(2,1)}), bf16[16,128,128]{2,1,0:T(8,128)(2,1)}, u32[]{:S(2)}, u32[]{:S(2)}) async-start(bf16[16,128,128]{2,1,0:T(8,128)(2,1)} %bitcast.50), calls=%async_computation.3 | async-start | bytes 1048576 | tf_op jit(solution)/shard_map/all_to_all | solution.py:269
  133.3 0.4 collective-permute-start.3
  133.7 2.6 %fusion.3 = (bf16[2,128,1024]{2,1,0:T(8,128)(2,1)}, bf16[2,128,1024]{2,1,0:T(8,128)(2,1)}) fusion(bf16[2,128,1024]{2,1,0:T(8,128)(2,1)} %collective-permute-done.12, bf16[2,4,128,1024]{3,2,1,0:T(8,128)(2,1)S(1)} %bitcast.48, s32[]{:T(128)S(6)} %select_n.47, bf16[2,128,1024]{2,1,0:T(8,128)(2,1)} %collective-permute-done.15, s32[]{:T(128)S(6)} %max.9), kind=kLoop, calls=%fused_computation.8 | loop fusion | flops 2097152 | bytes 3145736 | tf_op jit(solution)/shard_map/convert_element_type | solution.py:462
  136.3 16.7 %collective-permute-start.13 = (bf16[2,128,1024]{2,1,0:T(8,128)(2,1)}, bf16[2,128,1024]{2,1,0:T(8,128)(2,1)}, u32[]{:S(2)}, u32[]{:S(2)}) collective-permute-start(bf16[2,128,1024]{2,1,0:T(8,128)(2,1)} %get-tuple-element.28), channel_id=1, source_target_pairs={{0,8},{2,10},{4,12},{6,14},{8,16},{10,18},{12,20},{14,22},{16,24},... | collective-permute-start | bytes 1572872 | tf_op jit(solution)/shard_map/ppermute | solution.py:464
  153.0 1.3 collective-permute-start.16
  154.3 0.7 copy-done.4
  155.0 9.9 %query_grad.1 = bf16[512,2048]{1,0:T(8,128)(2,1)} custom-call(s32[1]{0:T(128)} %bitcast.me_ref, bf16[512,2048]{1,0:T(8,128)(2,1)} %get-tuple-element.16.g_ref, bf16[512,2048]{1,0:T(8,128)(2,1)} %v_ref.5, bf16[512,2048]{1,0:T(8,128)(2,1)} %k_ref.5, bf16[1024,128]{1,0:T(8,128)(2,1)} %get-tuple-element.21.s_ref, bf16[1024,128]{1,0:T(8,128)(2,1)} %copy-done.4), custom_call_target="tpu_custom_call" | custom-call | flops 2147483648 | bytes 8388608 | tf_op jit(solution)/shard_map/query_grad/pallas_call | solution.py:440
  164.8 14.0 %key_value_grad.1 = (bf16[512,2048]{1,0:T(8,128)(2,1)}, bf16[512,2048]{1,0:T(8,128)(2,1)}) custom-call(bf16[512,2048]{1,0:T(8,128)(2,1)} %q_ref.5, bf16[512,2048]{1,0:T(8,128)(2,1)} %k_ref.5, bf16[512,2048]{1,0:T(8,128)(2,1)} %v_ref.5, bf16[512,2048]{1,0:T(8,128)(2,1)} %get-tuple-element.16.g_ref, bf16[2048,128]{1,0:T(8,128)(2,1)} %bitcast.10.a_ref), custom_call_target="tpu_custom_call" | custom-call | flops 4294967296 | bytes 12582912 | tf_op jit(solution)/shard_map/key_value_grad/pallas_call | solution.py:234
  178.9 1.5 fusion.4
  180.4 0.1 select_bitcast_fusion.1
  180.5 1.0 pad_maximum_fusion
  (28 shorter events, 0.1 us)
Async XLA Ops:
  0.6 35.9 %copy-start = (f32[16,128,128]{2,1,0:T(8,128)S(1)}, f32[16,128,128]{2,1,0:T(8,128)}, u32[]{:S(2)}) copy-start(f32[16,128,128]{2,1,0:T(8,128)} %param.11) | copy-start | bytes 3145732
  0.6 26.5 %collective-permute-start.7 = (bf16[512,1024]{1,0:T(8,128)(2,1)}, bf16[512,1024]{1,0:T(8,128)(2,1)}, u32[]{:S(2)}, u32[]{:S(2)}) collective-permute-start(bf16[512,1024]{1,0:T(8,128)(2,1)} %refs_0_.1), channel_id=1, source_target_pairs={{0,4},{2,6},{4,0},{6,2},{8,12},{10,14},{12,8},{14,10},{16,20},{18,... | collective-permute-start | bytes 3145736 | tf_op jit(solution)/shard_map/ppermute | solution.py:480
  14.0 44.9 %collective-permute-start.1 = (bf16[512,2048]{1,0:T(8,128)(2,1)}, bf16[512,2048]{1,0:T(8,128)(2,1)S(1)}, u32[]{:S(2)}, u32[]{:S(2)}) collective-permute-start(bf16[512,2048]{1,0:T(8,128)(2,1)} %get-tuple-element.18), channel_id=1, source_target_pairs={{0,2},{2,0},{4,6},{6,4},{8,10},{10,8},{12,14},{14,12},{16,18},{18,... | collective-permute-start | bytes 6291464 | tf_op jit(solution)/shard_map/ppermute | solution.py:480
  20.7 8.2 %collective-permute-start.2 = (bf16[1024,128]{1,0:T(8,128)(2,1)}, bf16[1024,128]{1,0:T(8,128)(2,1)S(1)}, u32[]{:S(2)}, u32[]{:S(2)}) collective-permute-start(bf16[1024,128]{1,0:T(8,128)(2,1)} %get-tuple-element.20), channel_id=1, source_target_pairs={{0,2},{2,0},{4,6},{6,4},{8,10},{10,8},{12,14},{14,12},{16,18},{18,... | collective-permute-start | bytes 786440 | tf_op jit(solution)/shard_map/ppermute | solution.py:480
  21.2 30.0 %collective-permute-start = (bf16[512,1024]{1,0:T(8,128)(2,1)}, bf16[512,1024]{1,0:T(8,128)(2,1)}, u32[]{:S(2)}, u32[]{:S(2)}) collective-permute-start(bf16[512,1024]{1,0:T(8,128)(2,1)} %refs_0_.1), channel_id=1, source_target_pairs={{0,1},{1,0},{2,3},{3,2},{4,5},{5,4},{6,7},{7,6},{8,9},{9,8},{10,11... | collective-permute-start | bytes 3145736 | tf_op jit(solution)/shard_map/ppermute | solution.py:483
  27.2 41.9 %collective-permute-start.8 = (bf16[512,1024]{1,0:T(8,128)(2,1)}, bf16[512,1024]{1,0:T(8,128)(2,1)}, u32[]{:S(2)}, u32[]{:S(2)}) collective-permute-start(bf16[512,1024]{1,0:T(8,128)(2,1)} %collective-permute-done.7.refs_4_), channel_id=1, source_target_pairs={{0,1},{1,0},{2,3},{3,2},{4,5},{5,4},{6,7},{7,6},{8,9},{9,8},{10,11... | collective-permute-start | bytes 3145736 | tf_op jit(solution)/shard_map/ppermute | solution.py:483
  28.9 30.0 %copy-start.3 = (bf16[1024,128]{1,0:T(8,128)(2,1)}, bf16[1024,128]{1,0:T(8,128)(2,1)S(1)}, u32[]{:S(2)}) copy-start(bf16[1024,128]{1,0:T(8,128)(2,1)S(1)} %collective-permute-done.2.oth_ref) | copy-start | bytes 786436
  30.7 14.2 %all-to-all-start = ((bf16[8,128,128]{2,1,0:T(8,128)(2,1)}), bf16[8,128,128]{2,1,0:T(8,128)(2,1)}, u32[]{:S(2)}, u32[]{:S(2)}) async-start(bf16[8,128,128]{2,1,0:T(8,128)(2,1)} %bitcast.51), calls=%async_computation | async-start | bytes 524288 | tf_op jit(solution)/shard_map/all_to_all | solution.py:489
  46.5 12.3 %all-to-all-start.1 = ((bf16[8,128,128]{2,1,0:T(8,128)(2,1)}), bf16[8,128,128]{2,1,0:T(8,128)(2,1)}, u32[]{:S(2)}, u32[]{:S(2)}) async-start(bf16[8,128,128]{2,1,0:T(8,128)(2,1)} %bitcast.52), calls=%async_computation.1 | async-start | bytes 524288 | tf_op jit(solution)/shard_map/all_to_all | solution.py:492
  50.6 35.6 %collective-permute-start.5 = (bf16[512,1024]{1,0:T(8,128)(2,1)}, bf16[512,1024]{1,0:T(8,128)(2,1)}, u32[]{:S(2)}, u32[]{:S(2)}) collective-permute-start(bf16[512,1024]{1,0:T(8,128)(2,1)} %refs_0_.1), channel_id=1, source_target_pairs={{0,2},{2,0},{4,6},{6,4},{8,10},{10,8},{12,14},{14,12},{16,18},{18,... | collective-permute-start | bytes 3145736 | tf_op jit(solution)/shard_map/ppermute | solution.py:480
  50.7 35.6 %collective-permute-start.9 = (bf16[512,1024]{1,0:T(8,128)(2,1)}, bf16[512,1024]{1,0:T(8,128)(2,1)}, u32[]{:S(2)}, u32[]{:S(2)}) collective-permute-start(bf16[512,1024]{1,0:T(8,128)(2,1)} %collective-permute-done.7.refs_4_), channel_id=1, source_target_pairs={{0,2},{2,0},{4,6},{6,4},{8,10},{10,8},{12,14},{14,12},{16,18},{18,... | collective-permute-start | bytes 3145736 | tf_op jit(solution)/shard_map/ppermute | solution.py:480
  51.2 35.1 %collective-permute-start.6 = (bf16[512,1024]{1,0:T(8,128)(2,1)}, bf16[512,1024]{1,0:T(8,128)(2,1)}, u32[]{:S(2)}, u32[]{:S(2)}) collective-permute-start(bf16[512,1024]{1,0:T(8,128)(2,1)} %collective-permute-done.far_ref.refs_1_), channel_id=1, source_target_pairs={{0,2},{2,0},{4,6},{6,4},{8,10},{10,8},{12,14},{14,12},{16,18},{18,... | collective-permute-start | bytes 3145736 | tf_op jit(solution)/shard_map/ppermute | solution.py:480
  58.8 1.3 copy-start.2
  65.1 21.5 %collective-permute-start.4 = (bf16[2,512,512]{2,1,0:T(8,128)(2,1)}, bf16[2,512,512]{2,1,0:T(8,128)(2,1)S(1)}, u32[]{:S(2)}, u32[]{:S(2)}) collective-permute-start(bf16[2,512,512]{2,1,0:T(8,128)(2,1)} %get-tuple-element.27), channel_id=1, source_target_pairs={{0,4},{2,6},{4,0},{6,2},{8,12},{10,14},{12,8},{14,10},{16,20},{18,... | collective-permute-start | bytes 3145736 | tf_op jit(solution)/shard_map/ppermute | solution.py:480
  69.1 17.5 %collective-permute-start.10 = (bf16[512,1024]{1,0:T(8,128)(2,1)}, bf16[512,1024]{1,0:T(8,128)(2,1)S(1)}, u32[]{:S(2)}, u32[]{:S(2)}) collective-permute-start(bf16[512,1024]{1,0:T(8,128)(2,1)} %collective-permute-done.8.refs_5_), channel_id=1, source_target_pairs={{0,2},{2,0},{4,6},{6,4},{8,10},{10,8},{12,14},{14,12},{16,18},{18,... | collective-permute-start | bytes 3145736 | tf_op jit(solution)/shard_map/ppermute | solution.py:480
  81.1 43.2 %all-to-all-start.2 = ((bf16[16,128,128]{2,1,0:T(8,128)(2,1)}), bf16[16,128,128]{2,1,0:T(8,128)(2,1)}, u32[]{:S(2)}, u32[]{:S(2)}) async-start(bf16[16,128,128]{2,1,0:T(8,128)(2,1)} %bitcast.53), calls=%async_computation.2 | async-start | bytes 1048576 | tf_op jit(solution)/shard_map/all_to_all | solution.py:268
  86.6 1.0 copy-start.5
  86.6 1.3 copy-start.6
  97.5 17.7 %copy-start.1 = (bf16[2,512,1024]{2,1,0:T(8,128)(2,1)S(1)}, bf16[2,512,1024]{2,1,0:T(8,128)(2,1)}, u32[]{:S(2)}) copy-start(bf16[2,512,1024]{2,1,0:T(8,128)(2,1)} %quad_weight.1) | copy-start | bytes 6291460
  99.8 15.3 %collective-permute-start.11 = (bf16[2,128,1024]{2,1,0:T(8,128)(2,1)}, bf16[2,128,1024]{2,1,0:T(8,128)(2,1)}, u32[]{:S(2)}, u32[]{:S(2)}) collective-permute-start(bf16[2,128,1024]{2,1,0:T(8,128)(2,1)} %get-tuple-element.32), channel_id=1, source_target_pairs={{0,8},{2,10},{4,12},{6,14},{1,9},{3,11},{5,13},{7,15}} | collective-permute-start | bytes 1572872 | tf_op jit(solution)/shard_map/ppermute | solution.py:464
  104.1 11.0 %collective-permute-start.14 = (bf16[2,128,1024]{2,1,0:T(8,128)(2,1)}, bf16[2,128,1024]{2,1,0:T(8,128)(2,1)}, u32[]{:S(2)}, u32[]{:S(2)}) collective-permute-start(bf16[2,128,1024]{2,1,0:T(8,128)(2,1)} %get-tuple-element.33), channel_id=1, source_target_pairs={{24,16},{26,18},{28,20},{30,22},{25,17},{27,19},{29,21},{31,23}} | collective-permute-start | bytes 1572872 | tf_op jit(solution)/shard_map/ppermute | solution.py:465
  105.6 27.7 %copy-start.7 = (bf16[1024,128]{1,0:T(8,128)(2,1)S(1)}, bf16[1024,128]{1,0:T(8,128)(2,1)}, u32[]{:S(2)}) copy-start(bf16[1024,128]{1,0:T(8,128)(2,1)} %get-tuple-element.22) | copy-start | bytes 786436
  117.7 16.0 %collective-permute-start.12 = (bf16[2,128,1024]{2,1,0:T(8,128)(2,1)}, bf16[2,128,1024]{2,1,0:T(8,128)(2,1)}, u32[]{:S(2)}, u32[]{:S(2)}) collective-permute-start(bf16[2,128,1024]{2,1,0:T(8,128)(2,1)} %get-tuple-element.30), channel_id=1, source_target_pairs={{0,8},{2,10},{4,12},{6,14},{8,16},{10,18},{12,20},{14,22},{1,9},{3... | collective-permute-start | bytes 1572872 | tf_op jit(solution)/shard_map/ppermute | solution.py:464
  122.9 10.8 %collective-permute-start.15 = (bf16[2,128,1024]{2,1,0:T(8,128)(2,1)}, bf16[2,128,1024]{2,1,0:T(8,128)(2,1)}, u32[]{:S(2)}, u32[]{:S(2)}) collective-permute-start(bf16[2,128,1024]{2,1,0:T(8,128)(2,1)} %get-tuple-element.31), channel_id=1, source_target_pairs={{16,8},{18,10},{20,12},{22,14},{24,16},{26,18},{28,20},{30,22},{17... | collective-permute-start | bytes 1572872 | tf_op jit(solution)/shard_map/ppermute | solution.py:465
  126.9 38.0 %all-to-all-start.3 = ((bf16[16,128,128]{2,1,0:T(8,128)(2,1)}), bf16[16,128,128]{2,1,0:T(8,128)(2,1)}, u32[]{:S(2)}, u32[]{:S(2)}) async-start(bf16[16,128,128]{2,1,0:T(8,128)(2,1)} %bitcast.50), calls=%async_computation.3 | async-start | bytes 1048576 | tf_op jit(solution)/shard_map/all_to_all | solution.py:269
  133.3 21.0 %collective-permute-start.3 = (bf16[1024,128]{1,0:T(8,128)(2,1)S(1)}, bf16[1024,128]{1,0:T(8,128)(2,1)S(1)}, u32[]{:S(2)}, u32[]{:S(2)}) collective-permute-start(bf16[1024,128]{1,0:T(8,128)(2,1)S(1)} %copy-done.7), channel_id=1, source_target_pairs={{0,2},{2,0},{4,6},{6,4},{8,10},{10,8},{12,14},{14,12},{16,18},{18,... | collective-permute-start | bytes 786440 | tf_op jit(solution)/shard_map/ppermute | solution.py:480
  136.3 42.6 %collective-permute-start.13 = (bf16[2,128,1024]{2,1,0:T(8,128)(2,1)}, bf16[2,128,1024]{2,1,0:T(8,128)(2,1)}, u32[]{:S(2)}, u32[]{:S(2)}) collective-permute-start(bf16[2,128,1024]{2,1,0:T(8,128)(2,1)} %get-tuple-element.28), channel_id=1, source_target_pairs={{0,8},{2,10},{4,12},{6,14},{8,16},{10,18},{12,20},{14,22},{16,24},... | collective-permute-start | bytes 1572872 | tf_op jit(solution)/shard_map/ppermute | solution.py:464
  153.0 25.9 %collective-permute-start.16 = (bf16[2,128,1024]{2,1,0:T(8,128)(2,1)}, bf16[2,128,1024]{2,1,0:T(8,128)(2,1)}, u32[]{:S(2)}, u32[]{:S(2)}) collective-permute-start(bf16[2,128,1024]{2,1,0:T(8,128)(2,1)} %get-tuple-element.29), channel_id=1, source_target_pairs={{8,0},{10,2},{12,4},{14,6},{16,8},{18,10},{20,12},{22,14},{24,16},... | collective-permute-start | bytes 1572872 | tf_op jit(solution)/shard_map/ppermute | solution.py:465
  154.3 0.7 copy-start.4
